TPU v7x, 256 devices: a whole 4x4x8 slice. The times are simulated.
256 devices in a mesh: row: 4 (over x), col: 32 (over z, y), depth: 2 (over core).
Axes of the slice: x: 4, y: 4, z: 8, core: 2. Of those that a mesh axis runs over, the one named last changes fastest.
Arguments:
- xmat: bfloat16 [8192, 8192], P('row', ('col', 'depth'))
- mask_x: int32 [64, 64], P('row', ('col', 'depth')), may hold values from 0 to 1, as said below
- mask_sq: int32 [64, 64], P('row', ('col', 'depth')), may hold values from 0 to 1, as said below
- mask_out: int32 [64, 64], P('row', ('col', 'depth')), may hold values from 0 to 1, as said below
Outputs:
- new_iterate: bfloat16 [8192, 8192], P('row', ('col', 'depth'))
Inputs may be any that keep to these rules, and one draw needn't show every extreme that they name: `mask_x`: 0 or 1 for each block; every diagonal block is 1; in each aligned group of 16 block rows (rows 0 to 15, 16 to 31 and so on) every block column holds at most 4 ones, and block column 0 holds exactly 4 in every group. `mask_sq`: 0 or 1 for each block; every diagonal block is 1. `mask_out`: 0 or 1 for each block; every diagonal block is 1.
All inputs are finite; a program needn't handle non-finite values.
Results may differ from a plain program's by a relative error of at most 0.013.
Values may be sent and summed in bfloat16 or wider, within the bound.
A program may use at most 128 MiB of HBM per device.

v0:
```python
import jax
import jax.numpy as jnp
from jax import lax
from jax.experimental import pallas as pl
from jax.experimental.pallas import tpu as pltpu
from jax.sharding import PartitionSpec as P

BS = 128
RB = 16
SLOTS = 4
NX, NY, NZ = 4, 4, 8
NC = NY * NZ
HALF = BS // 2
RA = 192
RZ = SLOTS * BS - RA
B0 = 2 * NC * RA
ZERO = B0 + 2 * NC * RZ
ROWS = RB * BS
QS = (0, 2, 6, 10, 14)
QL = (2, 4, 4, 4, 2)
TILES = ((0, 2), (2, 4), (6, 8), (14, 2))
TR = 8
MSGS = 144

PARTS = ((0, 96), (96, 96), (0, 160), (160, 160))

ORDER = (
    -4, -52, -107, -77, -68, -116, -75, -45, -36, -84, -109, -43, -100, -20, -11, -13, 3, 51,
    -28, -60, -3, -5, 106, 76, -99, -85, -106, -78, 67, 115, 44, 74, -67, -83, -74, -124, 35,
    -37, 83, 108, 42, -110, -101, -69, -117, -92, -115, 99, 19, 10, 12, -19, -35, -14, -21, 128,
    27, 59, 2, 4, -27, -59, -29, 98, 84, 105, 77, -105, -79, -70, -86, 36, -38, 66, 82, 73, -73,
    -82, 109, 18, -102, -111, -18, -66, -118, 100, 123, 34, 13, -15, 26, 20, -26, 68, 116, -93,
    -125, 58, 28, -58, -30, -42, -61, -10, -53, -2, 91, 114, -123, 104, 78, -71, -97, -113,
    -114, -87, 69, 85, 37, -39, -46, 72, -80, 101, 81, 110, 17, -112, -103, -94, -119, -81, 129,
    25, 14, -25, -51, 65, 117, -90, 57, 29, -31, 41, 60, -41, -62, 92, 124, 9, 52, -9, -54, -6,
    1, 38, 70, 122, -1, -95, -34, -57, 45, -47, -40, -22, 96, 112, 79, -72, -65, 111, 24, -120,
    -32, -104, -98, -91, 102, 113, -122, -121, 50, 30, -50, -17, 40, 61, -63, 93, 86, 8, 53,
    -55, -16, 0, 5, 89, 118, -7, -8, -127, -126, 33, 46, -48, -33, 130, 94, 80, 56, 39, 31, 21,
    -23, 71, 119, -96, -128, -88, 49, -49, 62, -64, 64, 121, 16, -24, -89, 54, -56, 15, 6, 103,
    120, 7, 47, 32, 97, 126, 22, 90, 125, 48, 63, 23, 55, 95, 127, 88, 87,
)


def a_off(core, z, y):
    return pl.multiple_of(((core * NZ + z) * NY + y) * RA, HALF)


def b_off(core, y, z):
    return pl.multiple_of(B0 + ((core * NY + y) * NZ + z) * RZ, HALF)


def kernel(mx_hbm, msq_hbm, mo_hbm, x_hbm, out_ref, mx, msq, mo, x_ref, panel, xc, sb, acc,
           at_v, ct_v, at_s, ct_s, send_sem, recv_sem, local_sem):
    x = lax.axis_index("row")
    c = lax.axis_index("col")
    d = lax.axis_index("depth")
    z, y = c // NY, c % NY
    e = 1 - d

    def yy(k):
        return (y + (k + NY)) % NY

    def zz(k):
        return (z + (k + NZ)) % NZ

    def xx(k):
        return (x + (k + NX)) % NX

    def dev(dx=0, dy=0, dz=0, core=None):
        return {
            "row": xx(dx) if dx else x,
            "col": (zz(dz) if dz else z) * NY + (yy(dy) if dy else y),
            "depth": d if core is None else core,
        }

    yp, ym, zp, zm = dev(dy=1), dev(dy=-1), dev(dz=1), dev(dz=-1)
    xp, xm, x2, sib = dev(dx=1), dev(dx=-1), dev(dx=2), dev(core=e)
    y2, zpp, zmm = dev(dy=2), dev(dz=2), dev(dz=-2)
    partners = (zp, zm, yp, ym, zpp, zmm, y2, xp, xm, x2, sib)

    barrier = pltpu.get_barrier_semaphore()
    for partner in partners:
        pl.semaphore_signal(
            barrier, inc=1, device_id=partner, device_id_type=pl.DeviceIdType.MESH
        )

    inputs = [
        pltpu.make_async_copy(src, dst, local_sem.at[2 + n])
        for n, (src, dst) in enumerate(
            ((mx_hbm, mx), (msq_hbm, msq), (mo_hbm, mo), (x_hbm, x_ref))
        )
    ]
    for made in inputs:
        made.start()
    panel[pl.ds(ZERO, HALF)] = jnp.zeros((HALF, BS), jnp.bfloat16)
    for made in inputs:
        made.wait()

    count = jnp.int32(0)
    index = [jnp.int32(0)] * SLOTS
    lane = lax.broadcasted_iota(jnp.int32, (1, 128), 1)
    abase = a_off(d, z, y) // HALF
    bbase = b_off(d, y, z) // HALF
    entry = jnp.full((1, 128), ZERO // HALF, jnp.int32)
    for i in range(RB):
        keep = jnp.minimum(mx[i], 1)
        for s in range(SLOTS):
            here = jnp.maximum(1 - jnp.abs(count - s), 0)
            index[s] = index[s] + i * keep * here
        for h in range(2):
            g = 2 * count + h
            low = jnp.minimum(jnp.maximum(3 - g, 0), 1)
            at = low * (abase + g) + (1 - low) * (bbase + g - 3)
            at = keep * at + (1 - keep) * (ZERO // HALF)
            entry = jnp.where(lane == 2 * i + h, at, entry)
        count = count + keep
    column = jnp.full((1, 128), 2 * NC, jnp.int32)
    for s in range(SLOTS):
        there = jnp.minimum(jnp.maximum(count - s, 0), 1)
        k = there * (x * RB + index[s]) + (1 - there) * (2 * NC)
        column = jnp.where(lane == s, k, column)
    at_v[2 * c + d] = entry
    for core in range(2):
        at_v[2 * NC + core] = jnp.full((1, 128), ZERO // HALF, jnp.int32)
    ct_v[x] = column
    for s in range(SLOTS):
        for h in range(2):
            g = 2 * s + h
            piece = x_ref[pl.ds(index[s] * BS + h * HALF, HALF)]
            base = a_off(d, z, y) + HALF * g if g < 3 else b_off(d, y, z) + HALF * (g - 3)
            panel[pl.ds(pl.multiple_of(base, HALF), HALF)] = piece
            xc[pl.ds(pl.multiple_of(x * (SLOTS * BS) + g * HALF, HALF), HALF)] = piece

    pl.semaphore_wait(barrier, len(partners))

    names = {}
    sent = {}
    together = {"s": "s", "x": "x", "c": "c", "ty": "ty", "tz": "tz", "t3": "t3", "t4": "t3"}

    def copy(name, src, dst, target):
        key = together.get(name[0], together.get(name[:2], name))
        if name[0] in "qf":
            key = name[0] + name[2:]
        m = names.setdefault(key, len(names))
        kind = {"s": 1, "q": 2, "f": 2, "t": 3, "c": 3}.get(name[0], 0)
        made = pltpu.make_async_remote_copy(
            src_ref=src, dst_ref=dst, send_sem=send_sem.at[kind], recv_sem=recv_sem.at[m],
            device_id=target, device_id_type=pl.DeviceIdType.MESH,
        )
        return made, kind

    def send(name, ref, target):
        made, kind = copy(name, ref, ref, target)
        made.start()
        sent[kind] = sent.get(kind, 0) + ref.shape[0]

    def recv(name, ref, target):
        copy(name, ref, ref, target)[0].wait_recv()

    def pa(core, z_, y_, first=0, rows=RA):
        return panel.at[pl.ds(pl.multiple_of(a_off(core, z_, y_) + first, 16), rows)]

    def pb(core, y_, z_, first=0, rows=RZ):
        return panel.at[pl.ds(pl.multiple_of(b_off(core, y_, z_) + first, 16), rows)]

    def share(name, ref_of):
        send("s" + name, ref_of(d), sib)

    def entries(y_):
        return at_v.at[pl.ds(pl.multiple_of((z * NY + y_) * 2, 2), 2)]

    def table(z_):
        return at_v.at[pl.ds(pl.multiple_of(z_ * (2 * NY), 2), 2 * NY)]

    def chunk(part, v, k, core=None):
        core = d if core is None else core
        first, rows = PARTS[part]
        if part < 2:
            return pa(core, zz(k), yy(v), first, rows)
        return pb(core, yy(v), zz(k), first, rows)

    def step_of(part, v, k):
        far = part % 2
        if (k != 0) if part < 2 else (v == 0):
            if k < 0 or (k == 4 and not far):
                return (v, k + 1 if k < 0 else -3), zp
            return (v, k - 1), zm
        if v < 0 or (v == 2 and not far):
            return (v + 1 if v < 0 else -1, k), yp
        return (v - 1, k), ym

    def name_of(part, v, k):
        return f"{part},{v},{k}"

    def send_chunk(part, v, k):
        (pv, pk), target = step_of(part, v, k)
        send(name_of(part, v, k), chunk(part, pv, pk), target)

    def recv_chunk(part, v, k):
        recv(name_of(part, v, k), chunk(part, v, k), step_of(part, v, k)[1])
        arrived(part, v, k)

    here = {}

    def arrived(part, v, k):
        group = (part // 2, v, k)
        here[group] = here.get(group, 0) + 1
        if here[group] == 2 and part < 2:
            share(f"a{v},{k}", lambda core: pa(core, zz(k), yy(v)))
        elif here[group] == 2:
            share(f"b{v},{k}", lambda core: pb(core, yy(v), zz(k)))

    for part in range(4):
        arrived(part, 0, 0)
    send("t0", at_v.at[2 * c + d], sib)
    own = xc.at[pl.ds(pl.multiple_of(x * (SLOTS * BS), BS), SLOTS * BS)]
    for name, target in (("x+", xp), ("x-", xm), ("x2", x2)):
        send("c" + name, ct_v.at[x], target)
        send(name, own, target)
    started = False
    for n in ORDER:
        if n < 128:
            m = n if n >= 0 else -1 - n
            place = (m // 32, m // 8 % 4 - 1, m % 8 - 3)
            if n >= 0 and not started:
                started = True
                recv("t0", at_v.at[2 * c + e], sib)
                for name, target in (("ty+", yp), ("ty-", ym), ("ty2", y2)):
                    send(name, entries(y), target)
            if n >= 0:
                recv_chunk(*place)
            else:
                send_chunk(*place)
        elif n == 128:
            recv("ty", at_v.at[pl.ds(0, 3 * 2)], yp)
            for name, target in (("tz+", zp), ("tz-", zm), ("tzz+", zpp), ("tzz-", zmm)):
                send(name, table(z), target)
        elif n == 129:
            recv("tz", at_v.at[pl.ds(0, 4 * 2 * NY)], zp)
            send("t3+", table(zz(-1)), zpp)
            send("t3-", table(zz(1)), zmm)
            send("t4", table(zz(-2)), zpp)
        else:
            recv("t3", at_v.at[pl.ds(0, 3 * 2 * NY)], zpp)
    recv("c", ct_v.at[pl.ds(0, 3)], xp)
    recv("x", xc.at[pl.ds(0, 3 * SLOTS * BS)], xp)
    tables = [
        pltpu.make_async_copy(at_v, at_s, local_sem.at[0]),
        pltpu.make_async_copy(ct_v, ct_s, local_sem.at[1]),
    ]
    for made in tables:
        made.start()
    recv("s", panel.at[pl.ds(0, NC * SLOTS * BS)], sib)
    for made in tables:
        made.wait()

    def block(k, i):
        halves = [panel[pl.ds(at_s[k, 0, 2 * i + h] * HALF, HALF)] for h in range(2)]
        return jnp.concatenate(halves, axis=0)

    def tile(rows, columns):
        return jnp.concatenate(
            [jnp.concatenate([block(k, i) for k in columns], axis=1) for i in rows], axis=0
        )

    def masked(flag, values):
        return jnp.where(jnp.full(values.shape, flag, jnp.int32) != 0, values, 0.0)

    def s_ref(group_, q, half=None):
        first, rows = QS[q] * BS, QL[q] * BS
        if half is not None:
            rows //= 2
            first += half * rows
        return sb.at[pl.ds(pl.multiple_of(group_ * ROWS + first, BS), rows)]

    for first, count in TILES:
        rows = [first + i for i in range(count)]

        def pair(p, carry):
            columns = [ct_s[p // 2, 0, (p % 2) * 2 + j] for j in range(2)]
            term = jnp.dot(
                tile(rows, columns),
                xc[pl.ds(pl.multiple_of(p * 2 * BS, BS), 2 * BS)],
                preferred_element_type=jnp.float32,
            )
            spot = pl.ds(0, count * BS)
            acc[spot] = jnp.where(p == 0, term, acc[spot] + term)
            return carry

        lax.fori_loop(0, NX * SLOTS // 2, pair, 0)
        for i, row in enumerate(rows):
            part = masked(msq[row], acc[pl.ds(i * BS, BS)])
            sb[pl.ds(pl.multiple_of(x * ROWS + row * BS, BS), BS)] = part.astype(jnp.bfloat16)
        for q in range(len(QS)):
            if first <= QS[q] < first + count:
                send(f"q+{q}", s_ref(x, q), xp)
                send(f"q-{q}", s_ref(x, q), xm)

    acc[...] = jnp.zeros_like(acc)

    def cube(group_, first, count):
        w = sb[pl.ds(pl.multiple_of(group_ * ROWS + first * BS, BS), count * BS)]
        columns = [group_ * RB + first + k for k in range(count)]

        def some(ig, carry):
            spot = pl.ds(pl.multiple_of(ig * (TR * BS), BS), TR * BS)
            acc[spot] += jnp.dot(
                tile([ig * TR + i for i in range(TR)], columns), w,
                preferred_element_type=jnp.float32,
            )
            return carry

        lax.fori_loop(0, RB // TR, some, 0)

    def s_arrive(q):
        recv(f"q+{q}", sb.at[pl.ds(0, 2 * QL[q] * BS)], xp)
        send(f"f+{q}", s_ref(xx(-1), q, 0), xp)
        send(f"f-{q}", s_ref(xx(1), q, 1), xm)

    def s_last(q):
        recv(f"f+{q}", sb.at[pl.ds(0, QL[q] * BS)], xp)
        cube(xx(2), QS[q], QL[q])

    for q in range(len(QS)):
        cube(x, QS[q], QL[q])
    for q in range(len(QS)):
        s_arrive(q)
        if q < len(QS) - 2:
            cube(xx(-1), QS[q], QL[q])
            cube(xx(1), QS[q], QL[q])
    for k in (-1, 1):
        cube(xx(k), QS[-2], QL[-2] + QL[-1])
    for q in range(len(QS)):
        s_last(q)

    for i in range(RB):
        spot = pl.ds(i * BS, BS)
        kept = masked(mx[i], x_ref[spot].astype(jnp.float32))
        result = masked(mo[i], 1.5 * kept - 0.5 * acc[spot])
        out_ref[spot] = result.astype(jnp.bfloat16)

    for kind, buffer in ((0, panel), (1, panel), (2, sb), (3, at_v)):
        if kind in sent:
            whole = buffer.at[pl.ds(0, sent[kind])]
            pltpu.make_async_remote_copy(
                src_ref=whole, dst_ref=whole, send_sem=send_sem.at[kind], recv_sem=recv_sem.at[0],
                device_id=xp, device_id_type=pl.DeviceIdType.MESH,
            ).wait_send()


def body(xmat, mask_x, mask_sq, mask_out):
    hbm = pl.BlockSpec(memory_space=pltpu.HBM)
    vmem = pl.BlockSpec(memory_space=pltpu.VMEM)
    return pl.pallas_call(
        kernel,
        out_shape=jax.ShapeDtypeStruct(xmat.shape, jnp.bfloat16),
        in_specs=[hbm] * 4,
        out_specs=vmem,
        scratch_shapes=[
            pltpu.SMEM((RB,), jnp.int32),
            pltpu.SMEM((RB,), jnp.int32),
            pltpu.SMEM((RB,), jnp.int32),
            pltpu.VMEM((ROWS, BS), jnp.bfloat16),
            pltpu.VMEM((ZERO + HALF, BS), jnp.bfloat16),
            pltpu.VMEM((NX * SLOTS * BS, BS), jnp.bfloat16),
            pltpu.VMEM((NX * ROWS, BS), jnp.bfloat16),
            pltpu.VMEM((ROWS, BS), jnp.float32),
            pltpu.VMEM((2 * NC + 2, 1, 128), jnp.int32),
            pltpu.VMEM((NX, 1, 128), jnp.int32),
            pltpu.SMEM((2 * NC + 2, 1, 128), jnp.int32),
            pltpu.SMEM((NX, 1, 128), jnp.int32),
            pltpu.SemaphoreType.DMA((4,)),
            pltpu.SemaphoreType.DMA((MSGS,)),
            pltpu.SemaphoreType.DMA((6,)),
        ],
        compiler_params=pltpu.CompilerParams(
            collective_id=0, has_side_effects=True, vmem_limit_bytes=60 * 1024 * 1024
        ),
    )(mask_x.reshape(RB), mask_sq.reshape(RB), mask_out.reshape(RB), xmat)


def solution(mesh):
    placed = P("row", ("col", "depth"))
    return jax.shard_map(
        body, mesh=mesh, in_specs=(placed,) * 4, out_specs=placed, check_vma=False
    )
```

profile of v0, /device:TPU:1, one launch (start us, length us, event | category | flops | bytes accessed | tf_op | source)
XLA Modules:
  0.0 63.8 jit_solution(5647306304143426238)
XLA Ops:
  0.0 61.9 %shard_map.46 = bf16[2048,128]{1,0:T(8,128)(2,1)} custom-call(s32[16]{0:T(128)} %bitcast.3, s32[16]{0:T(128)} %bitcast.4, s32[16]{0:T(128)} %bitcast.5, bf16[2048,128]{1,0:T(8,128)(2,1)} %x_hbm.1), custom_call_target="tpu_custom_call" | custom-call | tf_op jit(solution)/shard_map/pallas_call | solution.py:354
  61.9 1.9 %copy.6 = bf16[2048,128]{1,0:T(8,128)(2,1)} copy(bf16[2048,128]{1,0:T(8,128)(2,1)} %shard_map.46) | data formatting | bytes 1048576
where the time goes:
time: 63.9 us; the launch traced here: 63.8 us
  Pallas kernels  61.9 us (97%)
  local copies, waits for them, and re-layouts  1.87 us (3%)
    pallas_call x1, Pallas kernels, body(): pl.pallas_call(kernel, out_shape=jax.ShapeDtypeStruct(xmat.shape, jnp.bfl...  61.9 us
    unnamed x1, local copies, waits for them, and re-layouts  1.87 us

commit v1 on v0

v1 whole, which is shorter than its diff:
```python
import jax
import jax.numpy as jnp
from jax import lax
from jax.experimental import pallas as pl
from jax.experimental.pallas import tpu as pltpu
from jax.sharding import PartitionSpec as P

BS = 128
RB = 16
SLOTS = 4
NX, NY, NZ = 4, 4, 8
NC = NY * NZ
PACK = SLOTS * BS
ZERO = 2 * NC * PACK
ROWS = RB * BS
QR = 2
QN = RB // QR
MSGS = 160

PARTS = ((0, 96), (96, 112), (208, 160), (368, 144))

ORDER = (
    -4, -52, -11, -109, -100, -75, -84, -77, -68, -43, -116, -13, -107, -36, -45, -20, 3, 10,
    -28, -3, -5, 51, -60, -51, 108, -101, -110, -117, -53, 99, 74, -74, -83, -10, 83, 76, -69,
    42, 67, 12, -14, -92, -67, 115, -124, 35, 44, 106, 19, -37, -19, -35, -78, -115, -99, -85,
    128, 27, 2, 4, -2, -106, 59, -61, -29, -46, -21, 50, 100, 109, -111, 116, -125, -118, 52,
    73, -66, -73, -102, -82, 68, -93, 82, 13, 9, 91, 36, 18, -18, -27, 123, 34, 66, 77, 114,
    -79, -70, -123, -86, 1, -1, -59, -34, 60, 98, 84, 105, -98, -114, 28, -30, 65, 124, -90, 45,
    -47, 72, -80, 20, -22, -62, 101, 117, 17, -17, 129, 26, -26, -105, 110, -119, -103, -112,
    -126, -54, -38, -15, 92, 81, 0, 78, -71, -87, -65, -81, 58, 122, -58, 69, 29, 33, -33, -42,
    85, 97, 46, 21, 79, -72, -23, -91, 113, -122, 89, 16, -24, -50, 61, -63, -6, 118, 25, 102,
    -25, -9, -8, 111, -120, -104, 125, 104, -113, -97, -127, -88, 70, 53, -55, 57, 37, 86, -39,
    -31, -48, 64, -89, 32, 14, 80, 71, 41, 22, -41, -96, -57, -95, -94, 130, 23, 62, 121, -64,
    90, 49, 5, -49, -7, 119, -128, 103, 24, -32, 54, -56, 112, 8, -121, -16, 38, -40, 96, 7, 30,
    126, 88, 40, 47, 87, 56, 63, 95, 48, 6, 127, 94, 31, 55, 15, 120, 39, 93,
)


def kernel(mx_hbm, msq_hbm, mo_hbm, x_hbm, out_ref, mx, msq, mo, x_ref, panel, xc, sb, acc,
           at_v, ct_v, at_s, ct_s, send_sem, recv_sem, local_sem):
    x = lax.axis_index("row")
    c = lax.axis_index("col")
    d = lax.axis_index("depth")
    z, y = c // NY, c % NY
    e = 1 - d

    def yy(k):
        return (y + (k + NY)) % NY

    def zz(k):
        return (z + (k + NZ)) % NZ

    def xx(k):
        return (x + (k + NX)) % NX

    def dev(dx=0, dy=0, dz=0, core=None):
        return {
            "row": xx(dx) if dx else x,
            "col": (zz(dz) if dz else z) * NY + (yy(dy) if dy else y),
            "depth": d if core is None else core,
        }

    yp, ym, zp, zm = dev(dy=1), dev(dy=-1), dev(dz=1), dev(dz=-1)
    xp, xm, x2, sib = dev(dx=1), dev(dx=-1), dev(dx=2), dev(core=e)
    y2, zpp, zmm = dev(dy=2), dev(dz=2), dev(dz=-2)
    partners = (zp, zm, yp, ym, zpp, zmm, y2, xp, xm, x2, sib)

    barrier = pltpu.get_barrier_semaphore()
    for partner in partners:
        pl.semaphore_signal(
            barrier, inc=1, device_id=partner, device_id_type=pl.DeviceIdType.MESH
        )

    inputs = [
        pltpu.make_async_copy(src, dst, local_sem.at[2 + n])
        for n, (src, dst) in enumerate(
            ((mx_hbm, mx), (msq_hbm, msq), (mo_hbm, mo), (x_hbm, x_ref))
        )
    ]
    for made in inputs:
        made.start()
    panel[pl.ds(ZERO, BS)] = jnp.zeros((BS, BS), jnp.bfloat16)
    for made in inputs:
        made.wait()

    count = jnp.int32(0)
    index = [jnp.int32(0)] * SLOTS
    lane = lax.broadcasted_iota(jnp.int32, (1, 128), 1)
    me = 2 * c + d
    entry = jnp.full((1, 128), ZERO // BS, jnp.int32)
    for i in range(RB):
        keep = jnp.minimum(mx[i], 1)
        for s in range(SLOTS):
            here = jnp.maximum(1 - jnp.abs(count - s), 0)
            index[s] = index[s] + i * keep * here
        at = keep * (me * SLOTS + count) + (1 - keep) * (ZERO // BS)
        entry = jnp.where(lane == i, at, entry)
        count = count + keep
    column = jnp.full((1, 128), 2 * NC, jnp.int32)
    for s in range(SLOTS):
        there = jnp.minimum(jnp.maximum(count - s, 0), 1)
        k = there * (x * RB + index[s]) + (1 - there) * (2 * NC)
        column = jnp.where(lane == s, k, column)
    at_v[2 * c + d] = entry
    for core in range(2):
        at_v[2 * NC + core] = jnp.full((1, 128), ZERO // BS, jnp.int32)
    ct_v[x] = column
    for s in range(SLOTS):
        piece = x_ref[pl.ds(index[s] * BS, BS)]
        panel[pl.ds(pl.multiple_of(me * PACK + s * BS, BS), BS)] = piece
        xc[pl.ds(pl.multiple_of(x * PACK + s * BS, BS), BS)] = piece

    pl.semaphore_wait(barrier, len(partners))

    names = {}
    sent = {}
    together = {"s": "s", "x": "x", "c": "c", "ty": "ty", "tz": "tz", "t3": "t3", "t4": "t3"}

    def copy(name, src, dst, target):
        key = together.get(name[0], together.get(name[:2], name))
        m = names.setdefault(key, len(names))
        kind = {"s": 1, "t": 3, "c": 3}.get(name[0], 0)
        made = pltpu.make_async_remote_copy(
            src_ref=src, dst_ref=dst, send_sem=send_sem.at[kind], recv_sem=recv_sem.at[m],
            device_id=target, device_id_type=pl.DeviceIdType.MESH,
        )
        return made, kind

    def send(name, ref, target):
        made, kind = copy(name, ref, ref, target)
        made.start()
        sent[kind] = sent.get(kind, 0) + ref.shape[0]

    def recv(name, ref, target):
        copy(name, ref, ref, target)[0].wait_recv()

    def pack(core, v, k, first=0, rows=PACK):
        column = (zz(k) * NY + yy(v)) * 2 + core
        return panel.at[pl.ds(pl.multiple_of(column * PACK + first, 16), rows)]

    def share(name, ref_of):
        send("s" + name, ref_of(d), sib)

    def entries(y_):
        return at_v.at[pl.ds(pl.multiple_of((z * NY + y_) * 2, 2), 2)]

    def table(z_):
        return at_v.at[pl.ds(pl.multiple_of(z_ * (2 * NY), 2), 2 * NY)]

    def chunk(part, v, k, core=None):
        return pack(d if core is None else core, v, k, *PARTS[part])

    def step_of(part, v, k):
        far = part % 2
        if (k != 0) if part < 2 else (v == 0):
            if k < 0 or (k == 4 and not far):
                return (v, k + 1 if k < 0 else -3), zp
            return (v, k - 1), zm
        if v < 0 or (v == 2 and not far):
            return (v + 1 if v < 0 else -1, k), yp
        return (v - 1, k), ym

    def name_of(part, v, k):
        return f"{part},{v},{k}"

    def send_chunk(part, v, k):
        (pv, pk), target = step_of(part, v, k)
        send(name_of(part, v, k), chunk(part, pv, pk), target)

    def recv_chunk(part, v, k):
        recv(name_of(part, v, k), chunk(part, v, k), step_of(part, v, k)[1])
        arrived(part, v, k)

    def arrived(part, v, k):
        share(f"{part},{v},{k}", lambda core: chunk(part, v, k, core))

    for part in range(4):
        arrived(part, 0, 0)
    send("t0", at_v.at[2 * c + d], sib)
    own = xc.at[pl.ds(pl.multiple_of(x * PACK, BS), PACK)]
    for name, target in (("x+", xp), ("x-", xm), ("x2", x2)):
        send("c" + name, ct_v.at[x], target)
        send(name, own, target)
    started = False
    for n in ORDER:
        if n < 128:
            m = n if n >= 0 else -1 - n
            place = (m // 32, m // 8 % 4 - 1, m % 8 - 3)
            if n >= 0 and not started:
                started = True
                recv("t0", at_v.at[2 * c + e], sib)
                for name, target in (("ty+", yp), ("ty-", ym), ("ty2", y2)):
                    send(name, entries(y), target)
            if n >= 0:
                recv_chunk(*place)
            else:
                send_chunk(*place)
        elif n == 128:
            recv("ty", at_v.at[pl.ds(0, 3 * 2)], yp)
            for name, target in (("tz+", zp), ("tz-", zm), ("tzz+", zpp), ("tzz-", zmm)):
                send(name, table(z), target)
        elif n == 129:
            recv("tz", at_v.at[pl.ds(0, 4 * 2 * NY)], zp)
            send("t3+", table(zz(-1)), zpp)
            send("t3-", table(zz(1)), zmm)
            send("t4", table(zz(-2)), zpp)
        else:
            recv("t3", at_v.at[pl.ds(0, 3 * 2 * NY)], zpp)
    recv("c", ct_v.at[pl.ds(0, 3)], xp)
    recv("x", xc.at[pl.ds(0, 3 * PACK)], xp)
    tables = [
        pltpu.make_async_copy(at_v, at_s, local_sem.at[0]),
        pltpu.make_async_copy(ct_v, ct_s, local_sem.at[1]),
    ]
    for made in tables:
        made.start()
    recv("s", panel.at[pl.ds(0, NC * PACK)], sib)
    for made in tables:
        made.wait()

    def block(k, i):
        return panel[pl.ds(at_s[k, 0, i] * BS, BS)]

    def tile(rows, columns):
        return jnp.concatenate(
            [jnp.concatenate([block(k, i) for k in columns], axis=1) for i in rows], axis=0
        )

    def masked(flag, values):
        return jnp.where(jnp.full(values.shape, flag, jnp.int32) != 0, values, 0.0)

    def s_ref(group_, q, half=None):
        first, rows = QS[q] * BS, QL[q] * BS
        if half is not None:
            rows //= 2
            first += half * rows
        return sb.at[pl.ds(pl.multiple_of(group_ * ROWS + first, BS), rows)]

    qrows = QR * BS
    first_q = len(names)

    def chunk_copy(group_, q, target, half=None):
        rows = qrows if half is None else qrows // 2
        first = 0 if half is None else half * rows
        ref = sb.at[pl.ds(pl.multiple_of(group_ * ROWS + q * qrows + first, BS), rows)]
        return pltpu.make_async_remote_copy(
            src_ref=ref, dst_ref=ref, send_sem=send_sem.at[2],
            recv_sem=recv_sem.at[first_q + q + (0 if half is None else QN)],
            device_id=target, device_id_type=pl.DeviceIdType.MESH,
        )

    def chunk_wait(q, forwarded):
        whole = sb.at[pl.ds(0, qrows if forwarded else 2 * qrows)]
        pltpu.make_async_remote_copy(
            src_ref=whole, dst_ref=whole, send_sem=send_sem.at[2],
            recv_sem=recv_sem.at[first_q + q + (QN if forwarded else 0)],
            device_id=xp, device_id_type=pl.DeviceIdType.MESH,
        ).wait_recv()

    kept = [ct_s[j // SLOTS, 0, j % SLOTS] for j in range(NX * SLOTS)]

    def square(q, carry):
        rows = [q * QR + i for i in range(QR)]
        total = None
        for p in range(NX * SLOTS // 2):
            term = jnp.dot(
                tile(rows, kept[2 * p : 2 * p + 2]),
                xc[pl.ds(p * 2 * BS, 2 * BS)],
                preferred_element_type=jnp.float32,
            )
            total = term if total is None else total + term
        for i, row in enumerate(rows):
            part = masked(msq[row], total[i * BS : (i + 1) * BS])
            sb[pl.ds(pl.multiple_of(x * ROWS + row * BS, BS), BS)] = part.astype(jnp.bfloat16)
        chunk_copy(x, q, xp).start()
        chunk_copy(x, q, xm).start()
        return carry

    lax.fori_loop(0, QN, square, 0)
    acc[...] = jnp.zeros_like(acc)

    def cube(group_, q):
        w = sb[pl.ds(pl.multiple_of(group_ * ROWS + q * qrows, BS), qrows)]
        columns = [group_ * RB + q * QR + k for k in range(QR)]
        acc[...] += jnp.dot(
            tile(range(RB), columns), w, preferred_element_type=jnp.float32
        )

    def own_chunk(q, carry):
        cube(x, q)
        return carry

    lax.fori_loop(0, QN, own_chunk, 0)

    def near_chunk(q, carry):
        chunk_wait(q, False)
        chunk_copy(xx(-1), q, xp, 0).start()
        chunk_copy(xx(1), q, xm, 1).start()

        def side(k, carry):
            cube(xx(2 * k - 1), q)
            return carry

        return lax.fori_loop(0, 2, side, carry)

    lax.fori_loop(0, QN, near_chunk, 0)

    def far_chunk(q, carry):
        chunk_wait(q, True)
        cube(xx(2), q)
        return carry

    lax.fori_loop(0, QN, far_chunk, 0)
    sent[2] = 3 * ROWS

    for i in range(RB):
        spot = pl.ds(i * BS, BS)
        own_x = masked(mx[i], x_ref[spot].astype(jnp.float32))
        result = masked(mo[i], 1.5 * own_x - 0.5 * acc[spot])
        out_ref[spot] = result.astype(jnp.bfloat16)

    for kind, buffer in ((0, panel), (1, panel), (2, sb), (3, at_v)):
        if kind in sent:
            whole = buffer.at[pl.ds(0, sent[kind])]
            pltpu.make_async_remote_copy(
                src_ref=whole, dst_ref=whole, send_sem=send_sem.at[kind], recv_sem=recv_sem.at[0],
                device_id=xp, device_id_type=pl.DeviceIdType.MESH,
            ).wait_send()


def body(xmat, mask_x, mask_sq, mask_out):
    hbm = pl.BlockSpec(memory_space=pltpu.HBM)
    vmem = pl.BlockSpec(memory_space=pltpu.VMEM)
    return pl.pallas_call(
        kernel,
        out_shape=jax.ShapeDtypeStruct(xmat.shape, jnp.bfloat16),
        in_specs=[hbm] * 4,
        out_specs=vmem,
        scratch_shapes=[
            pltpu.SMEM((RB,), jnp.int32),
            pltpu.SMEM((RB,), jnp.int32),
            pltpu.SMEM((RB,), jnp.int32),
            pltpu.VMEM((ROWS, BS), jnp.bfloat16),
            pltpu.VMEM((ZERO + BS, BS), jnp.bfloat16),
            pltpu.VMEM((NX * PACK, BS), jnp.bfloat16),
            pltpu.VMEM((NX * ROWS, BS), jnp.bfloat16),
            pltpu.VMEM((ROWS, BS), jnp.float32),
            pltpu.VMEM((2 * NC + 2, 1, 128), jnp.int32),
            pltpu.VMEM((NX, 1, 128), jnp.int32),
            pltpu.SMEM((2 * NC + 2, 1, 128), jnp.int32),
            pltpu.SMEM((NX, 1, 128), jnp.int32),
            pltpu.SemaphoreType.DMA((4,)),
            pltpu.SemaphoreType.DMA((MSGS,)),
            pltpu.SemaphoreType.DMA((6,)),
        ],
        compiler_params=pltpu.CompilerParams(
            collective_id=0, has_side_effects=True, vmem_limit_bytes=60 * 1024 * 1024
        ),
    )(mask_x.reshape(RB), mask_sq.reshape(RB), mask_out.reshape(RB), xmat)


def solution(mesh):
    placed = P("row", ("col", "depth"))
    return jax.shard_map(
        body, mesh=mesh, in_specs=(placed,) * 4, out_specs=placed, check_vma=False
    )
```

time: 63.9 us -> 61.7 us (0.966)
  Pallas kernels: 61.9 us -> 59.6 us
    pallas_call x1, Pallas kernels: 61.9 us -> 59.6 us  [body(): pl.pallas_call(kernel, out_shape=jax.ShapeDtypeStruct(xmat.shape, jnp.bfl...]
where the time goes in v1:
time: 61.7 us; the launch traced here: 61.5 us
  Pallas kernels  59.6 us (97%)
  local copies, waits for them, and re-layouts  1.87 us (3%)
    pallas_call x1, Pallas kernels, body(): pl.pallas_call(kernel, out_shape=jax.ShapeDtypeStruct(xmat.shape, jnp.bfl...  59.6 us
    unnamed x1, local copies, waits for them, and re-layouts  1.87 us

profile of v1, /device:TPU:1, one launch (start us, length us, event | category | flops | bytes accessed | tf_op | source)
XLA Modules:
  0.0 61.5 jit_solution(199965587325902504)
XLA Ops:
  0.0 59.6 %shard_map.46 = bf16[2048,128]{1,0:T(8,128)(2,1)} custom-call(s32[16]{0:T(128)} %bitcast.3, s32[16]{0:T(128)} %bitcast.4, s32[16]{0:T(128)} %bitcast.5, bf16[2048,128]{1,0:T(8,128)(2,1)} %x_hbm.1), custom_call_target="tpu_custom_call" | custom-call | tf_op jit(solution)/shard_map/pallas_call | solution.py:334
  59.7 1.9 %copy.6 = bf16[2048,128]{1,0:T(8,128)(2,1)} copy(bf16[2048,128]{1,0:T(8,128)(2,1)} %shard_map.46) | data formatting | bytes 1048576

commit v2 on v1

--- a/solution.py
+++ b/solution.py
@@ -15,7 +15,7 @@
 ROWS = RB * BS
 QR = 2
 QN = RB // QR
-MSGS = 160
+MSGS = 112
 
 PARTS = ((0, 96), (96, 112), (208, 160), (368, 144))
 
@@ -117,7 +117,7 @@
     together = {"s": "s", "x": "x", "c": "c", "ty": "ty", "tz": "tz", "t3": "t3", "t4": "t3"}
 
     def copy(name, src, dst, target):
-        key = together.get(name[0], together.get(name[:2], name))
+        key = together.get(name[0], together.get(name[:2], together.get(name, name)))
         m = names.setdefault(key, len(names))
         kind = {"s": 1, "t": 3, "c": 3}.get(name[0], 0)
         made = pltpu.make_async_remote_copy(
@@ -167,34 +167,46 @@
         (pv, pk), target = step_of(part, v, k)
         send(name_of(part, v, k), chunk(part, pv, pk), target)
 
-    def recv_chunk(part, v, k):
-        recv(name_of(part, v, k), chunk(part, v, k), step_of(part, v, k)[1])
-        arrived(part, v, k)
-
     def arrived(part, v, k):
         share(f"{part},{v},{k}", lambda core: chunk(part, v, k, core))
 
-    for part in range(4):
-        arrived(part, 0, 0)
+    def place(n):
+        return n // 32, n // 8 % 4 - 1, n % 8 - 3
+
+    runs = []
+    for n, before in zip(ORDER, (-1,) + ORDER):
+        if 0 <= n < 128:
+            if not 0 <= before < 128 or len(runs[-1]) == 2:
+                runs.append([])
+            runs[-1].append(place(n))
+    for number, run in enumerate(runs):
+        for one in run:
+            together[name_of(*one)] = f"run{number}"
+
     send("t0", at_v.at[2 * c + d], sib)
-    own = xc.at[pl.ds(pl.multiple_of(x * PACK, BS), PACK)]
-    for name, target in (("x+", xp), ("x-", xm), ("x2", x2)):
-        send("c" + name, ct_v.at[x], target)
-        send(name, own, target)
-    started = False
+    begun = 0
     for n in ORDER:
-        if n < 128:
-            m = n if n >= 0 else -1 - n
-            place = (m // 32, m // 8 % 4 - 1, m % 8 - 3)
-            if n >= 0 and not started:
-                started = True
+        if n < 0:
+            send_chunk(*place(-1 - n))
+        elif n < 128:
+            if begun == len(runs) or place(n) != runs[begun][0]:
+                continue
+            if begun == 0:
+                for part in range(4):
+                    arrived(part, 0, 0)
                 recv("t0", at_v.at[2 * c + e], sib)
                 for name, target in (("ty+", yp), ("ty-", ym), ("ty2", y2)):
                     send(name, entries(y), target)
-            if n >= 0:
-                recv_chunk(*place)
-            else:
-                send_chunk(*place)
+                own = xc.at[pl.ds(pl.multiple_of(x * PACK, BS), PACK)]
+                for name, target in (("x+", xp), ("x-", xm), ("x2", x2)):
+                    send("c" + name, ct_v.at[x], target)
+                    send(name, own, target)
+            run = runs[begun]
+            begun += 1
+            total = sum(PARTS[part][1] for part, _, _ in run)
+            recv(name_of(*run[0]), panel.at[pl.ds(0, total)], yp)
+            for one in run:
+                arrived(*one)
         elif n == 128:
             recv("ty", at_v.at[pl.ds(0, 3 * 2)], yp)
             for name, target in (("tz+", zp), ("tz-", zm), ("tzz+", zpp), ("tzz-", zmm)):
@@ -354,7 +366,7 @@
             pltpu.SemaphoreType.DMA((6,)),
         ],
         compiler_params=pltpu.CompilerParams(
-            collective_id=0, has_side_effects=True, vmem_limit_bytes=60 * 1024 * 1024
+            collective_id=0, has_side_effects=True, vmem_limit_bytes=53 * 1024 * 1024
         ),
     )(mask_x.reshape(RB), mask_sq.reshape(RB), mask_out.reshape(RB), xmat)
 

time: 61.7 us -> 60.1 us (0.974)
  Pallas kernels: 59.6 us -> 58.5 us
    pallas_call x1, Pallas kernels: 59.6 us -> 58.5 us  [body(): pl.pallas_call(kernel, out_shape=jax.ShapeDtypeStruct(xmat.shape, jnp.bfl...]
    unnamed x1 -> x7, local copies, waits for them, and re-layouts: 1.87 us -> 1.48 us
where the time goes in v2:
time: 60.1 us; the launch traced here: 60 us
  Pallas kernels  58.5 us (97%)
  local copies, waits for them, and re-layouts  1.48 us (2%)
    pallas_call x1, Pallas kernels, body(): pl.pallas_call(kernel, out_shape=jax.ShapeDtypeStruct(xmat.shape, jnp.bfl...  58.5 us
    unnamed x7, local copies, waits for them, and re-layouts  1.48 us

profile of v2, /device:TPU:1, one launch (start us, length us, event | category | flops | bytes accessed | tf_op | source)
XLA Modules:
  0.0 60.0 jit_solution(8208763335226763894)
XLA Ops:
  0.0 0.0 copy-start
  0.0 0.0 copy-start.1
  0.0 0.0 copy-start.2
  0.0 0.6 %copy-done = s32[16,1]{0,1:T(1,128)S(1)} copy-done((s32[16,1]{0,1:T(1,128)S(1)}, s32[16,1]{0,1:T(1,128)}, u32[]{:S(2)}) %copy-start) | copy-done | bytes 88
  0.7 0.0 copy-done.1
  0.7 0.0 copy-done.2
  0.7 58.5 %shard_map.46 = bf16[2048,128]{1,0:T(8,128)(2,1)S(1)} custom-call(s32[16]{0:T(128)S(1)} %bitcast.3, s32[16]{0:T(128)S(1)} %bitcast.4, s32[16]{0:T(128)S(1)} %bitcast.5, bf16[2048,128]{1,0:T(8,128)(2,1)} %x_hbm.1), custom_call_target="tpu_custom_call" | custom-call | tf_op jit(solution)/shard_map/pallas_call | solution.py:346
  59.2 0.8 %copy.6 = bf16[2048,128]{1,0:T(8,128)(2,1)} copy(bf16[2048,128]{1,0:T(8,128)(2,1)S(1)} %shard_map.46) | data formatting | bytes 1048576
Async XLA Ops:
  0.0 0.7 %copy-start = (s32[16,1]{0,1:T(1,128)S(1)}, s32[16,1]{0,1:T(1,128)}, u32[]{:S(2)}) copy-start(s32[16,1]{0,1:T(1,128)} %param.5) | copy-start | bytes 196
  0.0 0.7 %copy-start.1 = (s32[16,1]{0,1:T(1,128)S(1)}, s32[16,1]{0,1:T(1,128)}, u32[]{:S(2)}) copy-start(s32[16,1]{0,1:T(1,128)} %param.6) | copy-start | bytes 196
  0.0 0.7 %copy-start.2 = (s32[16,1]{0,1:T(1,128)S(1)}, s32[16,1]{0,1:T(1,128)}, u32[]{:S(2)}) copy-start(s32[16,1]{0,1:T(1,128)} %param.7) | copy-start | bytes 196

commit v3 on v2

--- a/solution.py
+++ b/solution.py
@@ -15,24 +15,24 @@
 ROWS = RB * BS
 QR = 2
 QN = RB // QR
-MSGS = 112
-
-PARTS = ((0, 96), (96, 112), (208, 160), (368, 144))
+MSGS = 102
+
+PARTS = ((0, 112), (112, 96), (208, 144), (352, 160))
 
 ORDER = (
-    -4, -52, -11, -109, -100, -75, -84, -77, -68, -43, -116, -13, -107, -36, -45, -20, 3, 10,
-    -28, -3, -5, 51, -60, -51, 108, -101, -110, -117, -53, 99, 74, -74, -83, -10, 83, 76, -69,
-    42, 67, 12, -14, -92, -67, 115, -124, 35, 44, 106, 19, -37, -19, -35, -78, -115, -99, -85,
-    128, 27, 2, 4, -2, -106, 59, -61, -29, -46, -21, 50, 100, 109, -111, 116, -125, -118, 52,
-    73, -66, -73, -102, -82, 68, -93, 82, 13, 9, 91, 36, 18, -18, -27, 123, 34, 66, 77, 114,
-    -79, -70, -123, -86, 1, -1, -59, -34, 60, 98, 84, 105, -98, -114, 28, -30, 65, 124, -90, 45,
-    -47, 72, -80, 20, -22, -62, 101, 117, 17, -17, 129, 26, -26, -105, 110, -119, -103, -112,
-    -126, -54, -38, -15, 92, 81, 0, 78, -71, -87, -65, -81, 58, 122, -58, 69, 29, 33, -33, -42,
-    85, 97, 46, 21, 79, -72, -23, -91, 113, -122, 89, 16, -24, -50, 61, -63, -6, 118, 25, 102,
-    -25, -9, -8, 111, -120, -104, 125, 104, -113, -97, -127, -88, 70, 53, -55, 57, 37, 86, -39,
-    -31, -48, 64, -89, 32, 14, 80, 71, 41, 22, -41, -96, -57, -95, -94, 130, 23, 62, 121, -64,
-    90, 49, 5, -49, -7, 119, -128, 103, 24, -32, 54, -56, 112, 8, -121, -16, 38, -40, 96, 7, 30,
-    126, 88, 40, 47, 87, 56, 63, 95, 48, 6, 127, 94, 31, 55, 15, 120, 39, 93,
+    -4, -52, -11, -77, -84, -100, -75, -109, -116, -43, -36, -13, -107, -68, -20, -45, 51, -60,
+    -51, -53, 3, 10, -28, -3, 76, -85, -78, -69, 83, 74, -74, 99, 108, -117, -110, -101, 42, 35,
+    -35, 115, -124, 12, -14, -37, 67, 19, 106, 44, -92, -19, -115, -106, -67, -99, -83, 128, 59,
+    50, 52, -61, -54, 27, -27, -29, 2, -2, 84, 77, -70, -79, 68, 73, -82, -73, -66, -93, 116,
+    109, -125, -111, -86, 100, 34, 13, 123, 18, -18, -50, 91, 36, 60, -62, 114, 105, 66, -105,
+    -91, -114, -102, -123, 53, -55, 26, -26, 82, 98, 28, -30, -46, -21, -38, 1, -1, 81, 69, 78,
+    -87, 72, -65, -80, 124, 65, -90, 17, -17, -59, -10, 110, -119, -112, -103, -118, -5, -15,
+    129, 49, 92, 85, 61, 54, 104, 90, -97, -113, -71, -81, 113, 29, 25, -25, -34, -42, 45, 101,
+    -47, 122, 0, 20, -22, 64, 86, 37, 79, -72, -88, -39, -63, 89, 16, 118, -24, 111, -104, -120,
+    -89, -98, 58, -58, 102, 117, 4, -6, -126, -31, 9, -9, 14, 96, 112, 24, -32, -121, -127,
+    -122, 46, -48, 33, -33, 70, -95, 80, 21, -23, 41, -41, -49, 130, 38, 71, -40, -96, -94, 87,
+    23, 62, -64, 57, -57, 103, 119, -128, 5, -7, -56, 8, -16, -8, 88, 30, 125, 31, 47, 32, 97,
+    120, 22, 40, 94, 39, 48, 126, 63, 95, 56, 121, 6, 15, 93, 55, 7, 127,
 )
 
 

time: 60.1 us -> 59.6 us (level)
  no operation moved by 1% of the time
where the time goes in v3:
time: 59.6 us; the launch traced here: 59.4 us
  Pallas kernels  57.9 us (97%)
  local copies, waits for them, and re-layouts  1.48 us (2%)
    pallas_call x1, Pallas kernels, body(): pl.pallas_call(kernel, out_shape=jax.ShapeDtypeStruct(xmat.shape, jnp.bfl...  57.9 us
    unnamed x7, local copies, waits for them, and re-layouts  1.48 us

profile of v3, /device:TPU:1, one launch (start us, length us, event | category | flops | bytes accessed | tf_op | source)
XLA Modules:
  0.0 59.4 jit_solution(11834782336792346005)
XLA Ops:
  0.0 0.0 copy-start
  0.0 0.0 copy-start.1
  0.0 0.0 copy-start.2
  0.0 0.6 %copy-done = s32[16,1]{0,1:T(1,128)S(1)} copy-done((s32[16,1]{0,1:T(1,128)S(1)}, s32[16,1]{0,1:T(1,128)}, u32[]{:S(2)}) %copy-start) | copy-done | bytes 88
  0.7 0.0 copy-done.1
  0.7 0.0 copy-done.2
  0.7 57.9 %shard_map.46 = bf16[2048,128]{1,0:T(8,128)(2,1)S(1)} custom-call(s32[16]{0:T(128)S(1)} %bitcast.3, s32[16]{0:T(128)S(1)} %bitcast.4, s32[16]{0:T(128)S(1)} %bitcast.5, bf16[2048,128]{1,0:T(8,128)(2,1)} %x_hbm.1), custom_call_target="tpu_custom_call" | custom-call | tf_op jit(solution)/shard_map/pallas_call | solution.py:346
  58.6 0.8 %copy.6 = bf16[2048,128]{1,0:T(8,128)(2,1)} copy(bf16[2048,128]{1,0:T(8,128)(2,1)S(1)} %shard_map.46) | data formatting | bytes 1048576
Async XLA Ops:
  0.0 0.7 %copy-start = (s32[16,1]{0,1:T(1,128)S(1)}, s32[16,1]{0,1:T(1,128)}, u32[]{:S(2)}) copy-start(s32[16,1]{0,1:T(1,128)} %param.5) | copy-start | bytes 196
  0.0 0.7 %copy-start.1 = (s32[16,1]{0,1:T(1,128)S(1)}, s32[16,1]{0,1:T(1,128)}, u32[]{:S(2)}) copy-start(s32[16,1]{0,1:T(1,128)} %param.6) | copy-start | bytes 196
  0.0 0.7 %copy-start.2 = (s32[16,1]{0,1:T(1,128)S(1)}, s32[16,1]{0,1:T(1,128)}, u32[]{:S(2)}) copy-start(s32[16,1]{0,1:T(1,128)} %param.7) | copy-start | bytes 196

commit v4 on v3

--- a/solution.py
+++ b/solution.py
@@ -322,13 +322,21 @@
         cube(xx(2), q)
         return carry
 
-    lax.fori_loop(0, QN, far_chunk, 0)
+    lax.fori_loop(0, QN - 1, far_chunk, 0)
     sent[2] = 3 * ROWS
 
     for i in range(RB):
         spot = pl.ds(i * BS, BS)
         own_x = masked(mx[i], x_ref[spot].astype(jnp.float32))
-        result = masked(mo[i], 1.5 * own_x - 0.5 * acc[spot])
+        acc[spot] = 1.5 * own_x - 0.5 * acc[spot]
+    chunk_wait(QN - 1, True)
+    last = xx(2)
+    w = sb[pl.ds(pl.multiple_of(last * ROWS + (QN - 1) * qrows, BS), qrows)]
+    columns = [last * RB + (QN - 1) * QR + k for k in range(QR)]
+    term = jnp.dot(tile(range(RB), columns), w, preferred_element_type=jnp.float32)
+    for i in range(RB):
+        spot = pl.ds(i * BS, BS)
+        result = masked(mo[i], acc[spot] - 0.5 * term[i * BS : (i + 1) * BS])
         out_ref[spot] = result.astype(jnp.bfloat16)
 
     for kind, buffer in ((0, panel), (1, panel), (2, sb), (3, at_v)):

time: 59.6 us -> 59.3 us (level)
  no operation moved by 1% of the time
where the time goes in v4:
time: 59.3 us; the launch traced here: 59.2 us
  Pallas kernels  57.7 us (97%)
  local copies, waits for them, and re-layouts  1.48 us (2%)
    pallas_call x1, Pallas kernels, body(): pl.pallas_call(kernel, out_shape=jax.ShapeDtypeStruct(xmat.shape, jnp.bfl...  57.7 us
    unnamed x7, local copies, waits for them, and re-layouts  1.48 us

profile of v4, /device:TPU:1, one launch (start us, length us, event | category | flops | bytes accessed | tf_op | source)
XLA Modules:
  0.0 59.2 jit_solution(722669117596146235)
XLA Ops:
  0.0 0.0 copy-start
  0.0 0.0 copy-start.1
  0.0 0.0 copy-start.2
  0.0 0.6 %copy-done = s32[16,1]{0,1:T(1,128)S(1)} copy-done((s32[16,1]{0,1:T(1,128)S(1)}, s32[16,1]{0,1:T(1,128)}, u32[]{:S(2)}) %copy-start) | copy-done | bytes 88
  0.7 0.0 copy-done.1
  0.7 0.0 copy-done.2
  0.7 57.7 %shard_map.46 = bf16[2048,128]{1,0:T(8,128)(2,1)S(1)} custom-call(s32[16]{0:T(128)S(1)} %bitcast.3, s32[16]{0:T(128)S(1)} %bitcast.4, s32[16]{0:T(128)S(1)} %bitcast.5, bf16[2048,128]{1,0:T(8,128)(2,1)} %x_hbm.1), custom_call_target="tpu_custom_call" | custom-call | tf_op jit(solution)/shard_map/pallas_call | solution.py:354
  58.4 0.8 %copy.6 = bf16[2048,128]{1,0:T(8,128)(2,1)} copy(bf16[2048,128]{1,0:T(8,128)(2,1)S(1)} %shard_map.46) | data formatting | bytes 1048576
Async XLA Ops:
  0.0 0.7 %copy-start = (s32[16,1]{0,1:T(1,128)S(1)}, s32[16,1]{0,1:T(1,128)}, u32[]{:S(2)}) copy-start(s32[16,1]{0,1:T(1,128)} %param.5) | copy-start | bytes 196
  0.0 0.7 %copy-start.1 = (s32[16,1]{0,1:T(1,128)S(1)}, s32[16,1]{0,1:T(1,128)}, u32[]{:S(2)}) copy-start(s32[16,1]{0,1:T(1,128)} %param.6) | copy-start | bytes 196
  0.0 0.7 %copy-start.2 = (s32[16,1]{0,1:T(1,128)S(1)}, s32[16,1]{0,1:T(1,128)}, u32[]{:S(2)}) copy-start(s32[16,1]{0,1:T(1,128)} %param.7) | copy-start | bytes 196

commit v5 on v4

--- a/solution.py
+++ b/solution.py
@@ -15,7 +15,7 @@
 ROWS = RB * BS
 QR = 2
 QN = RB // QR
-MSGS = 102
+MSGS = 80
 
 PARTS = ((0, 112), (112, 96), (208, 144), (352, 160))
 
@@ -176,7 +176,7 @@
     runs = []
     for n, before in zip(ORDER, (-1,) + ORDER):
         if 0 <= n < 128:
-            if not 0 <= before < 128 or len(runs[-1]) == 2:
+            if not 0 <= before < 128 or len(runs[-1]) == 4:
                 runs.append([])
             runs[-1].append(place(n))
     for number, run in enumerate(runs):

time: 59.3 us -> 59.3 us (level)
  no operation moved by 1% of the time
where the time goes in v5:
time: 59.3 us; the launch traced here: 59.2 us
  Pallas kernels  57.7 us (97%)
  local copies, waits for them, and re-layouts  1.48 us (2%)
    pallas_call x1, Pallas kernels, body(): pl.pallas_call(kernel, out_shape=jax.ShapeDtypeStruct(xmat.shape, jnp.bfl...  57.7 us
    unnamed x7, local copies, waits for them, and re-layouts  1.48 us

profile of v5, /device:TPU:1, one launch (start us, length us, event | category | flops | bytes accessed | tf_op | source)
XLA Modules:
  0.0 59.2 jit_solution(3861389283432385749)
XLA Ops:
  0.0 0.0 copy-start
  0.0 0.0 copy-start.1
  0.0 0.0 copy-start.2
  0.0 0.6 %copy-done = s32[16,1]{0,1:T(1,128)S(1)} copy-done((s32[16,1]{0,1:T(1,128)S(1)}, s32[16,1]{0,1:T(1,128)}, u32[]{:S(2)}) %copy-start) | copy-done | bytes 88
  0.7 0.0 copy-done.1
  0.7 0.0 copy-done.2
  0.7 57.7 %shard_map.46 = bf16[2048,128]{1,0:T(8,128)(2,1)S(1)} custom-call(s32[16]{0:T(128)S(1)} %bitcast.3, s32[16]{0:T(128)S(1)} %bitcast.4, s32[16]{0:T(128)S(1)} %bitcast.5, bf16[2048,128]{1,0:T(8,128)(2,1)} %x_hbm.1), custom_call_target="tpu_custom_call" | custom-call | tf_op jit(solution)/shard_map/pallas_call | solution.py:354
  58.4 0.8 %copy.6 = bf16[2048,128]{1,0:T(8,128)(2,1)} copy(bf16[2048,128]{1,0:T(8,128)(2,1)S(1)} %shard_map.46) | data formatting | bytes 1048576
Async XLA Ops:
  0.0 0.7 %copy-start = (s32[16,1]{0,1:T(1,128)S(1)}, s32[16,1]{0,1:T(1,128)}, u32[]{:S(2)}) copy-start(s32[16,1]{0,1:T(1,128)} %param.5) | copy-start | bytes 196
  0.0 0.7 %copy-start.1 = (s32[16,1]{0,1:T(1,128)S(1)}, s32[16,1]{0,1:T(1,128)}, u32[]{:S(2)}) copy-start(s32[16,1]{0,1:T(1,128)} %param.6) | copy-start | bytes 196
  0.0 0.7 %copy-start.2 = (s32[16,1]{0,1:T(1,128)S(1)}, s32[16,1]{0,1:T(1,128)}, u32[]{:S(2)}) copy-start(s32[16,1]{0,1:T(1,128)} %param.7) | copy-start | bytes 196
